TPU v7x, 256 devices: a whole 4x4x8 slice. The times are simulated.
256 devices in a mesh: seq: 32 (over y, z), chan: 8 (over x, core).
Axes of the slice: x: 4, y: 4, z: 8, core: 2. Of those that a mesh axis runs over, the one named last changes fastest.
Arguments:
- query_mr: bfloat16 [4096, 8192], P('seq', 'chan'), may hold values from -6 to 6
- key_mr: bfloat16 [4096, 8192], P('seq', 'chan'), may hold values from -6 to 6
- value_mr: bfloat16 [4096, 8192], P('seq', 'chan'), may hold values from -6 to 6
- query_li: bfloat16 [4096, 8192], P('seq', 'chan'), may hold values from -6 to 6
- key_li: bfloat16 [4096, 8192], P('seq', 'chan'), may hold values from -6 to 6
- cotangent: bfloat16 [4096, 8192], P('seq', 'chan'), may hold values from -40 to 40
- mr_filter: float32 [512, 128], P('chan'), may hold values from -3.535534 to 3.535534
- norm_gain: float32 [8192], P('chan'), may hold values from 0.1 to 1.9
- li_decay: float32 [512, 16], P('chan'), may hold values from 0.00012207031 to 0.03
- li_residue: float32 [512, 16], P('chan'), may hold values from -1 to 1
Outputs:
- out_li: bfloat16 [4096, 8192], P('seq', 'chan')
- grad_query_mr: bfloat16 [4096, 8192], P('seq', 'chan')
- grad_key_mr: bfloat16 [4096, 8192], P('seq', 'chan')
- grad_value_mr: bfloat16 [4096, 8192], P('seq', 'chan')
- grad_query_li: bfloat16 [4096, 8192], P('seq', 'chan')
- grad_key_li: bfloat16 [4096, 8192], P('seq', 'chan')
- grad_gain: float32 [8192], P('chan')
- grad_filter: float32 [512, 128], P('chan')
All inputs are finite; a program needn't handle non-finite values.
Results may differ from a plain program's by a relative error of at most 0.025.
Values may be sent and summed in bfloat16 or wider, within the bound.
A program may use at most 128 MiB of HBM per device.

v0:
```python
import jax
import jax.numpy as jnp
from jax import lax
from jax.sharding import PartitionSpec as P

D = 8192
G = 512
LBLK = 128
HIGHEST = lax.Precision.HIGHEST


def from_behind(value, axis, steps):
    count = lax.axis_size(axis)
    initial, last = (max(0, -steps), min(count, count - steps))
    return lax.ppermute(value, axis, [(source, source + steps) for source in range(initial, last)])


def toeplitz(edge_row):
    group_count, double_len = edge_row.shape
    block_len = double_len // 2
    cyclic = jnp.roll(jnp.flip(edge_row, -1), block_len + 1, axis=-1)
    repeated = jnp.tile(cyclic, (1, block_len))
    shaped = repeated[:, : block_len * (double_len - 1)].reshape(
        group_count, block_len, double_len - 1
    )
    return shaped[:, :, :block_len]


def combine_pair(earlier, latter):
    return (earlier[0] * latter[0], latter[1] + latter[0][..., None] * earlier[1])


def modal_parts(blocks, decays, residues, backward):
    block_len = blocks.shape[1]
    offsets = jnp.arange(block_len, dtype=jnp.float32)
    rate_col = decays[:, :, None]
    weights_res = residues * jnp.sqrt(2.0 * decays)
    fading = jnp.exp(-rate_col * offsets)
    filter_taps = jnp.einsum("gr,grd->gd", weights_res, fading, precision=HIGHEST)
    matrix = toeplitz(jnp.concatenate([jnp.zeros_like(filter_taps), filter_taps], -1))
    if backward:
        inside = jnp.einsum("gji,bjgc->bigc", matrix, blocks, precision=HIGHEST)
        weigh_in = fading
        weigh_out = weights_res[:, :, None] * jnp.exp(-rate_col * (block_len - offsets))
    else:
        inside = jnp.einsum("gij,bjgc->bigc", matrix, blocks, precision=HIGHEST)
        weigh_in = jnp.exp(-rate_col * (block_len - 1.0 - offsets))
        weigh_out = weights_res[:, :, None] * jnp.exp(-rate_col * (offsets + 1.0))
    states = jnp.einsum("grj,bjgc->bgrc", weigh_in, blocks, precision=HIGHEST)
    powers = jnp.broadcast_to(jnp.exp(-decays * block_len), (blocks.shape[0],) + decays.shape)
    running = lax.associative_scan(combine_pair, (powers, states), reverse=backward, axis=0)
    return (inside, weigh_out, running)


def modal_finish(inside, weigh_out, running, incoming, backward):
    powers, states = running
    if backward:
        prior_pow = jnp.concatenate([powers[1:], jnp.ones_like(powers[:1])], 0)
        prior_sum = jnp.concatenate([states[1:], jnp.zeros_like(states[:1])], 0)
    else:
        prior_pow = jnp.concatenate([jnp.ones_like(powers[:1]), powers[:-1]], 0)
        prior_sum = jnp.concatenate([jnp.zeros_like(states[:1]), states[:-1]], 0)
    entering = prior_sum + prior_pow[..., None] * incoming[None]
    return inside + jnp.einsum("gri,bgrc->bigc", weigh_out, entering, precision=HIGHEST)


def local_long(columns, decays, residues, backward):
    seq_len, chan_count = columns.shape
    group_size = D // G
    blocks = columns.reshape(seq_len // LBLK, LBLK, chan_count // group_size, group_size)
    inside, weigh_out, running = modal_parts(blocks, decays, residues, backward)
    incoming = jnp.zeros_like(running[1][0])
    return modal_finish(inside, weigh_out, running, incoming, backward).reshape(seq_len, chan_count)


def on_device(
    query_mr,
    key_mr,
    value_mr,
    query_li,
    key_li,
    cotangent,
    mr_filter,
    norm_gain,
    li_decay,
    li_residue,
):
    row_count, chan_count = query_mr.shape
    group_count, tap_count = mr_filter.shape
    group_size = chan_count // group_count
    block_count = row_count // tap_count
    grad_scale = float(row_count * lax.axis_size("seq")) ** (-0.5)
    taps_mr = mr_filter.astype(jnp.bfloat16)
    zero_taps = jnp.zeros_like(taps_mr)
    lower_band = toeplitz(jnp.concatenate([zero_taps, taps_mr], -1))
    upper_band = toeplitz(jnp.concatenate([taps_mr, zero_taps], -1))
    mixed_mr = (key_mr.astype(jnp.float32) * value_mr.astype(jnp.float32)).astype(jnp.bfloat16)
    rim_rows = from_behind(mixed_mr, "seq", 1)
    blocks = mixed_mr.reshape(block_count, tap_count, group_count, group_size)
    before = jnp.concatenate(
        [rim_rows.reshape(1, tap_count, group_count, group_size), blocks[:-1]], 0
    )
    conv_mr = jnp.einsum("gij,bjgc->bigc", lower_band, blocks, preferred_element_type=jnp.float32)
    conv_mr = conv_mr + jnp.einsum(
        "gij,bjgc->bigc", upper_band, before, preferred_element_type=jnp.float32
    )
    conv_mr = conv_mr.reshape(row_count, chan_count)
    out_mr = (query_mr.astype(jnp.float32) * conv_mr).astype(jnp.bfloat16)
    out_full = lax.optimization_barrier(out_mr).astype(jnp.float32)
    squares = lax.psum(jnp.sum(out_full * out_full, axis=1), "chan")
    inv_rms = lax.rsqrt(squares / D + 1e-06)[:, None]
    normed = out_full * inv_rms * norm_gain
    mixed_li = key_li.astype(jnp.float32) * normed
    cotan_full = cotangent.astype(jnp.float32)
    back_li = cotan_full * query_li.astype(jnp.float32)
    local_groups = group_count // lax.axis_size("seq")
    group_start = lax.axis_index("seq") * local_groups
    decays_here = lax.dynamic_slice_in_dim(li_decay, group_start, local_groups, 0)
    residues_here = lax.dynamic_slice_in_dim(li_residue, group_start, local_groups, 0)
    columns = lax.all_to_all(
        mixed_li.astype(jnp.bfloat16), "seq", split_axis=1, concat_axis=0, tiled=True
    ).astype(mixed_li.dtype)
    conv_li = lax.all_to_all(
        local_long(columns, decays_here, residues_here, False).astype(jnp.bfloat16),
        "seq",
        split_axis=0,
        concat_axis=1,
        tiled=True,
    ).astype(jnp.float32)
    grad_columns = lax.all_to_all(
        back_li.astype(jnp.bfloat16), "seq", split_axis=1, concat_axis=0, tiled=True
    ).astype(back_li.dtype)
    grad_mixed_li = lax.all_to_all(
        local_long(grad_columns, decays_here, residues_here, True),
        "seq",
        split_axis=0,
        concat_axis=1,
        tiled=True,
    )
    out_li = (query_li.astype(jnp.float32) * conv_li).astype(jnp.bfloat16)
    grad_query_li = (cotan_full * conv_li).astype(jnp.bfloat16)
    grad_key_li = (grad_mixed_li * normed).astype(jnp.bfloat16)
    grad_normed = grad_mixed_li * key_li.astype(jnp.float32)
    gain_part = jnp.sum(grad_normed * out_full * inv_rms, axis=0)
    weighted = grad_normed * norm_gain
    cross_dots = lax.psum(jnp.sum(weighted * out_full, axis=1), "chan")[:, None]
    grad_out_mr = inv_rms * weighted - out_full * inv_rms**3 * cross_dots / D
    grad_query_mr = (grad_out_mr * conv_mr).astype(jnp.bfloat16)
    back_mr = (grad_out_mr * query_mr.astype(jnp.float32)).astype(jnp.bfloat16)
    after_rim = from_behind(back_mr, "seq", -1)
    back_blocks = back_mr.reshape(block_count, tap_count, group_count, group_size)
    after_rows = jnp.concatenate(
        [back_blocks[1:], after_rim.reshape(1, tap_count, group_count, group_size)], 0
    )
    grad_mixed_mr = jnp.einsum(
        "gji,bjgc->bigc", lower_band, back_blocks, preferred_element_type=jnp.float32
    )
    grad_mixed_mr = grad_mixed_mr + jnp.einsum(
        "gji,bjgc->bigc", upper_band, after_rows, preferred_element_type=jnp.float32
    )
    grad_mixed_mr = grad_mixed_mr.reshape(row_count, chan_count)
    grad_key_mr = (grad_mixed_mr * value_mr.astype(jnp.float32)).astype(jnp.bfloat16)
    grad_value_mr = (grad_mixed_mr * key_mr.astype(jnp.float32)).astype(jnp.bfloat16)
    extended = jnp.concatenate([before, blocks], 1)
    gram_block = jnp.einsum(
        "bigc,bmgc->gim", back_blocks, extended, preferred_element_type=jnp.float32
    )
    flipped = jnp.flip(gram_block, -1)
    padded = jnp.pad(flipped, ((0, 0), (0, 0), (0, 1)))
    flattened = padded.reshape(group_count, -1)
    skewed = flattened[:, tap_count - 1 : tap_count - 1 + 2 * tap_count * tap_count]
    skewed = skewed.reshape(group_count, tap_count, 2 * tap_count)[:, :, :tap_count]
    filter_part = jnp.sum(skewed, axis=1)
    param_sums = (
        lax.psum(gain_part.astype(jnp.bfloat16), "seq").astype(jnp.float32),
        lax.psum(filter_part.astype(jnp.bfloat16), "seq").astype(jnp.float32),
    )
    grad_gain = param_sums[0] * grad_scale
    grad_filter = param_sums[1] * grad_scale
    return (
        out_li,
        grad_query_mr,
        grad_key_mr,
        grad_value_mr,
        grad_query_li,
        grad_key_li,
        grad_gain,
        grad_filter,
    )


def solution(mesh):
    in_specs = (
        P("seq", "chan"),
        P("seq", "chan"),
        P("seq", "chan"),
        P("seq", "chan"),
        P("seq", "chan"),
        P("seq", "chan"),
        P("chan", None),
        P("chan"),
        P("chan", None),
        P("chan", None),
    )
    out_specs = (
        P("seq", "chan"),
        P("seq", "chan"),
        P("seq", "chan"),
        P("seq", "chan"),
        P("seq", "chan"),
        P("seq", "chan"),
        P("chan"),
        P("chan", None),
    )
    return jax.shard_map(
        on_device, mesh=mesh, in_specs=in_specs, out_specs=out_specs, check_vma=False
    )
```

profile of v0, /device:TPU:32, one launch (start us, length us, event | category | flops | bytes accessed | tf_op | source)
XLA Modules:
  0.0 443.5 jit_solution(472008142492113452)
XLA Ops:
  0.7 1.1 copy.227
  1.8 1.1 copy.245
  2.9 0.8 fusion.24
  3.7 11.5 %all-to-all-start.2 = ((bf16[128,32,32]{0,2,1:T(8,128)(2,1)}), bf16[128,32,32]{0,2,1:T(8,128)(2,1)S(1)}, u32[]{:S(2)}, u32[]{:S(2)}) async-start(bf16[128,32,32]{0,2,1:T(8,128)(2,1)} %bitcast.30), calls=%async_computation.2 | async-start | bytes 524288 | tf_op jit(solution)/shard_map/all_to_all | solution.py:130
  15.2 1.1 copy.230
  16.3 1.1 copy.231
  17.6 3.4 collective-permute-start
  21.2 0.6 fusion.92
  25.0 0.7 copy.253
  25.8 0.7 copy.254
  26.5 0.7 slice_multiply_fusion
  27.3 0.7 fusion.97
  28.0 0.7 copy.252
  34.2 2.6 copy.273
  36.8 2.2 slice.458
  39.0 15.9 %reshape.167 = bf16[64,128,255]{2,1,0:T(8,128)(2,1)} reshape(bf16[64,32640]{1,0:T(8,128)(2,1)} %slice.458) | data formatting | bytes 8355840 | tf_op jit(solution)/shard_map/reshape | solution.py:23
  55.2 2.6 copy.274
  57.8 2.2 slice.460
  60.0 15.9 %reshape.169 = bf16[64,128,255]{2,1,0:T(8,128)(2,1)} reshape(bf16[64,32640]{1,0:T(8,128)(2,1)} %slice.460) | data formatting | bytes 8355840 | tf_op jit(solution)/shard_map/reshape | solution.py:23
  76.4 0.6 iota_subtract_fusion
  77.0 3.6 fusion.6
  81.2 0.7 multiply_add_fusion.4
  81.9 0.7 multiply_add_fusion.6
  82.6 0.7 slice_add_fusion
  83.3 0.7 fusion.95
  84.1 0.7 fusion.56
  85.5 0.7 add.314
  86.6 11.2 %pad.305 = f32[32,2,16,16]{2,3,0,1:T(8,128)S(1)} pad(f32[16,2,16,16]{2,3,0,1:T(8,128)} %add.314, f32[]{:T(128)} %constant.15.clone.1), padding=1_0_1x0_0_0x0_0_0x0_0_0 | pad | bytes 98308
  97.8 0.9 slice_add_fusion.2
  98.7 1.9 slice.444
  100.9 1.7 fusion.14
  102.6 0.9 copy.257
  103.5 8.9 %all-to-all-start.3 = ((f32[32,128,32]{1,2,0:T(8,128)}), f32[32,128,32]{1,2,0:T(8,128)S(1)}, u32[]{:S(2)}, u32[]{:S(2)}) async-start(f32[32,128,32]{1,2,0:T(8,128)} %bitcast.140), calls=%async_computation.3 | async-start | bytes 1048576 | tf_op jit(solution)/shard_map/all_to_all | solution.py:133
  112.4 2.9 fusion.8
  115.6 13.8 %psum.28 = f32[128]{0:T(128)S(1)} all-reduce(f32[128]{0:T(128)S(1)} %fusion.26), channel_id=1, replica_groups=mesh['seq'=32,'chan'=8] {'chan'}, use_global_device_ids=true, to_apply=%region_1.2 | all-reduce | flops 128 | bytes 1024 | tf_op jit(solution)/shard_map/psum | solution.py:110
  129.8 12.4 %psum.29 = f32[128]{0:T(128)S(1)} all-reduce(f32[128]{0:T(128)S(1)} %get-tuple-element.49), channel_id=1, replica_groups=mesh['seq'=32,'chan'=8] {'chan'}, use_global_device_ids=true, to_apply=%region_3.4 | all-reduce | flops 128 | bytes 1024 | tf_op jit(solution)/shard_map/psum | solution.py:146
  142.2 1.3 fusion.20
  143.4 1.8 copy.259
  145.2 9.5 %all-to-all-start = ((bf16[128,32,32]{0,2,1:T(8,128)(2,1)}), bf16[128,32,32]{0,2,1:T(8,128)(2,1)S(1)}, u32[]{:S(2)}, u32[]{:S(2)}) async-start(bf16[128,32,32]{0,2,1:T(8,128)(2,1)} %bitcast.141), calls=%async_computation | async-start | bytes 524288 | tf_op jit(solution)/shard_map/all_to_all | solution.py:120
  154.8 1.8 copy.263
  156.5 2.1 collective-permute-start.1
  158.7 5.5 %fusion.36 = f32[64,128,256]{2,1,0:T(8,128)} fusion(bf16[128,64,16]{0,2,1:T(8,128)(2,1)S(1)} %bitcast.138, bf16[1,128,64,16]{1,3,2,0:T(8,128)(2,1)S(1)} %bitcast.137, bf16[1,128,64,16]{1,3,2,0:T(8,128)(2,1)} %bitcast.55), kind=kOutput, calls=%fused_computation.53 | convolution fusion | flops 68157440 | bytes 9175040 | tf_op jit(solution)/shard_map/bigc,bmgc->gim/dot_general | solution.py:165
  164.2 67.4 %rev.14 = f32[64,128,256]{2,1,0:T(8,128)} reverse(f32[64,128,256]{2,1,0:T(8,128)} %fusion.36), dimensions={2} | reverse | bytes 16777216 | tf_op jit(solution)/shard_map/jit(_flip)/rev | solution.py:168
  231.5 9.6 %pad.177 = f32[64,128,257]{2,1,0:T(8,128)} pad(f32[64,128,256]{2,1,0:T(8,128)} %rev.14, f32[]{:T(128)} %constant.15.clone.1), padding=0_0x0_0x0_1 | pad | bytes 16809988 | tf_op jit(solution)/shard_map/jit(_pad)/pad | solution.py:169
  241.1 12.2 %reshape.180 = f32[64,32896]{1,0:T(8,128)} reshape(f32[64,128,257]{2,1,0:T(8,128)} %pad.177) | data formatting | bytes 16842752 | tf_op jit(solution)/shard_map/reshape | solution.py:170
  253.3 5.6 %slice.516 = f32[64,32768]{1,0:T(8,128)S(1)} slice(f32[64,32896]{1,0:T(8,128)} %reshape.180), slice={[0:64], [127:32895]} | slice | bytes 16777216 | tf_op jit(solution)/shard_map/slice | solution.py:171
  258.9 2.5 copy.276
  261.5 0.5 slice_reduce_fusion
  262.0 139.5 %all-reduce.49 = (bf16[1024]{0:T(1024)(128)(2,1)S(1)}, bf16[64,128]{1,0:T(8,128)(2,1)S(1)}) all-reduce(bf16[1024]{0:T(1024)(128)(2,1)S(1)} %get-tuple-element.48, bf16[64,128]{1,0:T(8,128)(2,1)S(1)} %slice_reduce_fusion), channel_id=1, replica_groups=mesh['seq'=32,'chan'=8] {'seq'}, use_global_device_ids=true, to_apply=%region_5.6 | all-reduce | flops 9216 | bytes 36864 | tf_op jit(solution)/shard_map/psum | solution.py:175
  401.5 0.6 convert_multiply_fusion.15
  402.1 0.6 convert_multiply_fusion.16
  402.7 2.2 fusion.4
  406.5 0.7 add.291
  407.5 11.2 %pad.303 = f32[32,2,16,16]{2,3,0,1:T(8,128)S(1)} pad(f32[16,2,16,16]{2,3,0,1:T(8,128)} %add.291, f32[]{:T(128)} %constant.15.clone.1), padding=1_0_1x0_0_0x0_0_0x0_0_0 | pad | bytes 98308
  418.8 1.3 fusion.52
  420.1 0.6 fusion.16
  420.8 0.7 copy.244
  421.5 9.1 %all-to-all-start.1 = ((bf16[32,128,32]{1,2,0:T(8,128)(2,1)}), bf16[32,128,32]{1,2,0:T(8,128)(2,1)S(1)}, u32[]{:S(2)}, u32[]{:S(2)}) async-start(bf16[32,128,32]{1,2,0:T(8,128)(2,1)} %bitcast.27), calls=%async_computation.1 | async-start | bytes 524288 | tf_op jit(solution)/shard_map/all_to_all | solution.py:123
  430.6 2.3 fusion.11
  433.1 0.9 copy.261
  433.9 0.8 copy.260
  434.8 6.9 %all-to-all-done.1 = bf16[32,128,32]{1,2,0:T(8,128)(2,1)S(1)} async-done(((bf16[32,128,32]{1,2,0:T(8,128)(2,1)}), bf16[32,128,32]{1,2,0:T(8,128)(2,1)S(1)}, u32[]{:S(2)}, u32[]{:S(2)}) %all-to-all-start.1) | async-done | bytes 262176 | tf_op jit(solution)/shard_map/all_to_all | solution.py:123
  441.8 0.9 copy.262
  442.7 0.8 copy.258
  (194 shorter events, 14.4 us)
Async XLA Ops:
  0.6 20.3 %copy-start.10 = (f32[64,16]{0,1:T(8,128)S(1)}, f32[64,16]{0,1:T(8,128)}, u32[]{:S(2)}) copy-start(f32[64,16]{0,1:T(8,128)} %param.19) | copy-start | bytes 12292
  0.6 20.3 %copy-start.9 = (f32[64,16]{0,1:T(8,128)S(1)}, f32[64,16]{0,1:T(8,128)}, u32[]{:S(2)}) copy-start(f32[64,16]{0,1:T(8,128)} %param.18) | copy-start | bytes 12292
  0.7 29.6 %copy-start.3 = (f32[64,128]{1,0:T(8,128)S(1)}, f32[64,128]{1,0:T(8,128)}, u32[]{:S(2)}) copy-start(f32[64,128]{1,0:T(8,128)} %param.16) | copy-start | bytes 98308
  2.9 30.5 %copy-start.1 = (bf16[128,1024]{1,0:T(8,128)(2,1)S(1)}, bf16[128,1024]{1,0:T(8,128)(2,1)}, u32[]{:S(2)}) copy-start(bf16[128,1024]{1,0:T(8,128)(2,1)} %param.10) | copy-start | bytes 786436
  3.7 29.9 %copy-start.2 = (bf16[128,1024]{1,0:T(8,128)(2,1)S(1)}, bf16[128,1024]{1,0:T(8,128)(2,1)}, u32[]{:S(2)}) copy-start(bf16[128,1024]{1,0:T(8,128)(2,1)} %param.14) | copy-start | bytes 786436
  3.7 76.9 %all-to-all-start.2 = ((bf16[128,32,32]{0,2,1:T(8,128)(2,1)}), bf16[128,32,32]{0,2,1:T(8,128)(2,1)S(1)}, u32[]{:S(2)}, u32[]{:S(2)}) async-start(bf16[128,32,32]{0,2,1:T(8,128)(2,1)} %bitcast.30), calls=%async_computation.2 | async-start | bytes 524288 | tf_op jit(solution)/shard_map/all_to_all | solution.py:130
  17.6 94.9 %collective-permute-start = (bf16[128,1024]{0,1:T(8,128)(2,1)S(1)}, bf16[128,1024]{0,1:T(8,128)(2,1)}, u32[]{:S(2)}, u32[]{:S(2)}) collective-permute-start(bf16[128,1024]{0,1:T(8,128)(2,1)S(1)} %fusion.22), channel_id=1, source_target_pairs={{0,8},{8,16},{16,24},{24,32},{32,40},{40,48},{48,56},{56,64},{64,7... | collective-permute-start | bytes 786440 | tf_op jit(solution)/shard_map/ppermute | solution.py:15
  21.8 7.3 %copy-start.6 = (f32[2,16]{1,0:T(2,128)}, f32[2,16]{1,0:T(2,128)S(1)}, u32[]{:S(2)}) copy-start(f32[2,16]{1,0:T(2,128)S(1)} %get-tuple-element.92) | copy-start | bytes 388
  33.4 67.1 %copy-start = (f32[2,128,255]{2,1,0:T(8,128)}, f32[2,128,255]{2,1,0:T(8,128)S(1)}, u32[]{:S(2)}) copy-start(f32[2,128,255]{2,1,0:T(8,128)S(1)} %reshape.172) | copy-start | bytes 783364
  85.1 15.8 %copy-start.7 = (f32[2,16]{1,0:T(2,128)S(1)}, f32[2,16]{1,0:T(2,128)}, u32[]{:S(2)}) copy-start(f32[2,16]{1,0:T(2,128)} %copy-done.6) | copy-start | bytes 388
  85.1 15.8 %copy-start.12 = (f32[128]{0:T(128)S(1)}, f32[128]{0:T(128)}, u32[]{:S(2)}) copy-start(f32[128]{0:T(128)} %iota_subtract_fusion) | copy-start | bytes 1540
  100.9 28.4 %copy-start.4 = (f32[1024]{0:T(1024)S(1)}, f32[1024]{0:T(1024)}, u32[]{:S(2)}) copy-start(f32[1024]{0:T(1024)} %param.17) | copy-start | bytes 12292
  103.5 25.9 %all-to-all-start.3 = ((f32[32,128,32]{1,2,0:T(8,128)}), f32[32,128,32]{1,2,0:T(8,128)S(1)}, u32[]{:S(2)}, u32[]{:S(2)}) async-start(f32[32,128,32]{1,2,0:T(8,128)} %bitcast.140), calls=%async_computation.3 | async-start | bytes 1048576 | tf_op jit(solution)/shard_map/all_to_all | solution.py:133
  145.2 259.7 %all-to-all-start = ((bf16[128,32,32]{0,2,1:T(8,128)(2,1)}), bf16[128,32,32]{0,2,1:T(8,128)(2,1)S(1)}, u32[]{:S(2)}, u32[]{:S(2)}) async-start(bf16[128,32,32]{0,2,1:T(8,128)(2,1)} %bitcast.141), calls=%async_computation | async-start | bytes 524288 | tf_op jit(solution)/shard_map/all_to_all | solution.py:120
  156.5 274.1 %collective-permute-start.1 = (bf16[128,1024]{0,1:T(8,128)(2,1)S(1)}, bf16[128,1024]{0,1:T(8,128)(2,1)}, u32[]{:S(2)}, u32[]{:S(2)}) collective-permute-start(bf16[128,1024]{0,1:T(8,128)(2,1)S(1)} %get-tuple-element.52), channel_id=1, source_target_pairs={{8,0},{16,8},{24,16},{32,24},{40,32},{48,40},{56,48},{64,56},{72,6... | collective-permute-start | bytes 786440 | tf_op jit(solution)/shard_map/ppermute | solution.py:15
  261.4 143.5 %copy-start.13 = (f32[128]{0:T(128)S(1)}, f32[128]{0:T(128)}, u32[]{:S(2)}) copy-start(f32[128]{0:T(128)} %iota_subtract_fusion.1) | copy-start | bytes 1540
  261.5 144.1 %copy-start.5 = (f32[2,16]{1,0:T(2,128)S(1)}, f32[2,16]{1,0:T(2,128)}, u32[]{:S(2)}) copy-start(f32[2,16]{1,0:T(2,128)} %get-tuple-element.82) | copy-start | bytes 388
  261.5 144.1 %copy-start.11 = (f32[2,16]{1,0:T(2,128)S(1)}, f32[2,16]{1,0:T(2,128)}, u32[]{:S(2)}) copy-start(f32[2,16]{1,0:T(2,128)} %get-tuple-element.89) | copy-start | bytes 388
  405.9 14.3 %copy-start.8 = (f32[2,16]{1,0:T(2,128)S(1)}, f32[2,16]{1,0:T(2,128)}, u32[]{:S(2)}) copy-start(f32[2,16]{1,0:T(2,128)} %copy-done.6) | copy-start | bytes 388
  421.5 20.2 %all-to-all-start.1 = ((bf16[32,128,32]{1,2,0:T(8,128)(2,1)}), bf16[32,128,32]{1,2,0:T(8,128)(2,1)S(1)}, u32[]{:S(2)}, u32[]{:S(2)}) async-start(bf16[32,128,32]{1,2,0:T(8,128)(2,1)} %bitcast.27), calls=%async_computation.1 | async-start | bytes 524288 | tf_op jit(solution)/shard_map/all_to_all | solution.py:123
where the time goes:
time: 451 us; the launch traced here: 444 us
  local copies, waits for them, and re-layouts  188 us (42%)
  blocking collectives  166 us (37%)
  starting transfers between devices  44.5 us (10%)
  matrix products  21.6 us (5%)
  other arithmetic  15.6 us (3%)
  waiting for transfers between devices  6.91 us (2%)
    psum x1, blocking collectives, on_device(): lax.psum(gain_part.astype(jnp.bfloat16), 'seq').astype(jnp.float32)  139 us
    rev x1, local copies, waits for them, and re-layouts, on_device(): flipped = jnp.flip(gram_block, -1)  67.4 us
    unnamed x57, local copies, waits for them, and re-layouts  43.6 us
    reshape x3, local copies, waits for them, and re-layouts, toeplitz(): repeated[:, :block_len * (double_len - 1)]  32.2 us
    psum x1, blocking collectives, on_device(): squares = lax.psum(jnp.sum(out_full * out_full, axis=1), 'chan')  13.8 us
    psum x1, blocking collectives, on_device(): cross_dots = lax.psum(jnp.sum(weighted * out_full, axis=1), 'chan')[:, None]  12.4 us
    reshape x1, local copies, waits for them, and re-layouts, on_device(): flattened = padded.reshape(group_count, -1)  12.2 us
    all_to_all x1, starting transfers between devices, on_device(): lax.all_to_all(back_li.astype(jnp.bfloat16), 'seq', split_axis=1, concat_...  11.5 us
  transfers between devices with their start and end apart: 6, of which 1 were waited for; matrix products, arithmetic and copies ran while one was open for 49% of the time, Pallas kernels for 0%

commit v1 on v0

--- a/solution.py
+++ b/solution.py
@@ -7,6 +7,12 @@
 G = 512
 LBLK = 128
 HIGHEST = lax.Precision.HIGHEST
+
+
+def gather_and_add(array, mesh_axis):
+    terms = lax.all_gather(array, mesh_axis, axis=0, tiled=False)
+    acc = terms.sum(axis=0)
+    return acc
 
 
 def from_behind(value, axis, steps):
@@ -172,7 +178,7 @@
     skewed = skewed.reshape(group_count, tap_count, 2 * tap_count)[:, :, :tap_count]
     filter_part = jnp.sum(skewed, axis=1)
     param_sums = (
-        lax.psum(gain_part.astype(jnp.bfloat16), "seq").astype(jnp.float32),
+        gather_and_add(gain_part.astype(jnp.bfloat16), "seq").astype(jnp.float32),
         lax.psum(filter_part.astype(jnp.bfloat16), "seq").astype(jnp.float32),
     )
     grad_gain = param_sums[0] * grad_scale

time: 451 us -> 499 us (1.11)
  blocking collectives: 166 us -> 214 us
    all_gather x0 -> x1, blocking collectives: none -> 50.1 us  [gather_and_add(): terms = lax.all_gather(array, mesh_axis, axis=0, tiled=False)]
    unnamed x57 -> x55, local copies, waits for them, and re-layouts: 43.6 us -> 43.6 us
  transfers between devices with their start and end apart: 6 -> 6, of which waited for: 1 -> 1; matrix products, arithmetic and copies ran while one was open for 49% -> 44% of each run, Pallas kernels for 0% -> 0%
where the time goes in v1:
time: 499 us; the launch traced here: 492 us
  blocking collectives  214 us (43%)
  local copies, waits for them, and re-layouts  188 us (38%)
  starting transfers between devices  44.3 us (9%)
  matrix products  21.6 us (4%)
  other arithmetic  15.6 us (3%)
  waiting for transfers between devices  6.91 us (1%)
    psum x1, blocking collectives, on_device(): lax.psum(filter_part.astype(jnp.bfloat16), 'seq').astype(jnp.float32)  138 us
    rev x1, local copies, waits for them, and re-layouts, on_device(): flipped = jnp.flip(gram_block, -1)  67.4 us
    all_gather x1, blocking collectives, gather_and_add(): terms = lax.all_gather(array, mesh_axis, axis=0, tiled=False)  50.1 us
    unnamed x55, local copies, waits for them, and re-layouts  43.6 us
    reshape x3, local copies, waits for them, and re-layouts, toeplitz(): repeated[:, :block_len * (double_len - 1)]  32.1 us
    psum x1, blocking collectives, on_device(): squares = lax.psum(jnp.sum(out_full * out_full, axis=1), 'chan')  13.8 us
    psum x1, blocking collectives, on_device(): cross_dots = lax.psum(jnp.sum(weighted * out_full, axis=1), 'chan')[:, None]  12.4 us
    reshape x1, local copies, waits for them, and re-layouts, on_device(): flattened = padded.reshape(group_count, -1)  12.2 us
  transfers between devices with their start and end apart: 6, of which 1 were waited for; matrix products, arithmetic and copies ran while one was open for 44% of the time, Pallas kernels for 0%

profile of v1, /device:TPU:32, one launch (start us, length us, event | category | flops | bytes accessed | tf_op | source)
XLA Modules:
  0.0 492.0 jit_solution(6958982823771989033)
XLA Ops:
  0.7 1.1 copy.323
  1.8 1.1 copy.341
  2.9 0.8 fusion.24
  3.7 11.5 %all-to-all-start.2 = ((bf16[128,32,32]{0,2,1:T(8,128)(2,1)}), bf16[128,32,32]{0,2,1:T(8,128)(2,1)S(1)}, u32[]{:S(2)}, u32[]{:S(2)}) async-start(bf16[128,32,32]{0,2,1:T(8,128)(2,1)} %bitcast.30), calls=%async_computation.2 | async-start | bytes 524288 | tf_op jit(solution)/shard_map/all_to_all | solution.py:136
  15.2 1.1 copy.326
  16.3 1.1 copy.327
  17.6 3.4 collective-permute-start
  21.2 0.6 fusion.92
  25.0 0.7 copy.349
  25.8 0.7 copy.350
  26.5 0.7 slice_multiply_fusion
  27.3 0.7 fusion.97
  28.0 0.7 copy.348
  34.2 2.6 copy.369
  36.8 2.2 slice.458
  39.0 15.9 %reshape.175 = bf16[64,128,255]{2,1,0:T(8,128)(2,1)} reshape(bf16[64,32640]{1,0:T(8,128)(2,1)} %slice.458) | data formatting | bytes 8355840 | tf_op jit(solution)/shard_map/reshape | solution.py:29
  55.2 2.6 copy.370
  57.8 2.2 slice.460
  60.0 15.8 %reshape.177 = bf16[64,128,255]{2,1,0:T(8,128)(2,1)} reshape(bf16[64,32640]{1,0:T(8,128)(2,1)} %slice.460) | data formatting | bytes 8355840 | tf_op jit(solution)/shard_map/reshape | solution.py:29
  76.4 0.6 iota_subtract_fusion
  76.9 3.6 fusion.6
  81.2 0.7 multiply_add_fusion.4
  81.9 0.7 multiply_add_fusion.6
  82.6 0.7 slice_add_fusion
  83.2 0.7 fusion.95
  84.1 0.7 fusion.56
  85.4 0.7 add.312
  86.6 11.2 %pad.305 = f32[32,2,16,16]{2,3,0,1:T(8,128)S(1)} pad(f32[16,2,16,16]{2,3,0,1:T(8,128)} %add.312, f32[]{:T(128)} %constant.15.clone.1), padding=1_0_1x0_0_0x0_0_0x0_0_0 | pad | bytes 98308
  97.8 0.9 slice_add_fusion.2
  98.6 1.8 slice.444
  100.9 1.7 fusion.14
  102.6 0.9 copy.353
  103.4 8.9 %all-to-all-start.3 = ((f32[32,128,32]{1,2,0:T(8,128)}), f32[32,128,32]{1,2,0:T(8,128)S(1)}, u32[]{:S(2)}, u32[]{:S(2)}) async-start(f32[32,128,32]{1,2,0:T(8,128)} %bitcast.140), calls=%async_computation.3 | async-start | bytes 1048576 | tf_op jit(solution)/shard_map/all_to_all | solution.py:139
  112.4 2.9 fusion.8
  115.5 13.8 %psum.21 = f32[128]{0:T(128)S(1)} all-reduce(f32[128]{0:T(128)S(1)} %fusion.26), channel_id=1, replica_groups=mesh['seq'=32,'chan'=8] {'chan'}, use_global_device_ids=true, to_apply=%region_1.2 | all-reduce | flops 128 | bytes 1024 | tf_op jit(solution)/shard_map/psum | solution.py:116
  129.7 12.4 %psum.22 = f32[128]{0:T(128)S(1)} all-reduce(f32[128]{0:T(128)S(1)} %get-tuple-element.65), channel_id=1, replica_groups=mesh['seq'=32,'chan'=8] {'chan'}, use_global_device_ids=true, to_apply=%region_3.4 | all-reduce | flops 128 | bytes 1024 | tf_op jit(solution)/shard_map/psum | solution.py:152
  142.1 1.3 fusion.20
  143.4 1.8 copy.355
  145.2 9.5 %all-to-all-start = ((bf16[128,32,32]{0,2,1:T(8,128)(2,1)}), bf16[128,32,32]{0,2,1:T(8,128)(2,1)S(1)}, u32[]{:S(2)}, u32[]{:S(2)}) async-start(bf16[128,32,32]{0,2,1:T(8,128)(2,1)} %bitcast.141), calls=%async_computation | async-start | bytes 524288 | tf_op jit(solution)/shard_map/all_to_all | solution.py:126
  154.7 50.1 %all-gather = bf16[32768]{0:T(1024)(128)(2,1)S(1)} all-gather(bf16[1024]{0:T(1024)(128)(2,1)S(1)} %get-tuple-element.64), channel_id=2, replica_groups=mesh['seq'=32,'chan'=8] {'seq'}, dimensions={0}, use_global_device_ids=true | all-gather | bytes 67584 | tf_op jit(solution)/shard_map/all_gather | solution.py:13
  204.9 1.8 copy.359
  206.7 1.9 collective-permute-start.1
  208.6 5.5 %fusion.36 = f32[64,128,256]{2,1,0:T(8,128)} fusion(bf16[128,64,16]{0,2,1:T(8,128)(2,1)S(1)} %bitcast.138, bf16[1,128,64,16]{1,3,2,0:T(8,128)(2,1)S(1)} %bitcast.137, bf16[1,128,64,16]{1,3,2,0:T(8,128)(2,1)} %bitcast.55), kind=kOutput, calls=%fused_computation.53 | convolution fusion | flops 68157440 | bytes 9175040 | tf_op jit(solution)/shard_map/bigc,bmgc->gim/dot_general | solution.py:171
  214.1 67.4 %rev.14 = f32[64,128,256]{2,1,0:T(8,128)} reverse(f32[64,128,256]{2,1,0:T(8,128)} %fusion.36), dimensions={2} | reverse | bytes 16777216 | tf_op jit(solution)/shard_map/jit(_flip)/rev | solution.py:174
  281.5 9.5 %pad.177 = f32[64,128,257]{2,1,0:T(8,128)} pad(f32[64,128,256]{2,1,0:T(8,128)} %rev.14, f32[]{:T(128)} %constant.15.clone.1), padding=0_0x0_0x0_1 | pad | bytes 16809988 | tf_op jit(solution)/shard_map/jit(_pad)/pad | solution.py:175
  291.0 12.2 %reshape.188 = f32[64,32896]{1,0:T(8,128)} reshape(f32[64,128,257]{2,1,0:T(8,128)} %pad.177) | data formatting | bytes 16842752 | tf_op jit(solution)/shard_map/reshape | solution.py:176
  303.2 5.6 %slice.516 = f32[64,32768]{1,0:T(8,128)S(1)} slice(f32[64,32896]{1,0:T(8,128)} %reshape.188), slice={[0:64], [127:32895]} | slice | bytes 16777216 | tf_op jit(solution)/shard_map/slice | solution.py:177
  308.8 2.5 copy.372
  311.9 138.1 %psum.23 = bf16[64,128]{1,0:T(8,128)(2,1)S(1)} all-reduce(bf16[64,128]{1,0:T(8,128)(2,1)S(1)} %slice_reduce_fusion), channel_id=1, replica_groups=mesh['seq'=32,'chan'=8] {'seq'}, use_global_device_ids=true, to_apply=%region_7.8 | all-reduce | flops 8192 | bytes 32768 | tf_op jit(solution)/shard_map/psum | solution.py:182
  450.0 0.6 convert_multiply_fusion.15
  450.6 0.6 convert_multiply_fusion.16
  451.2 2.2 fusion.4
  455.0 0.7 add.289
  456.1 11.2 %pad.303 = f32[32,2,16,16]{2,3,0,1:T(8,128)S(1)} pad(f32[16,2,16,16]{2,3,0,1:T(8,128)} %add.289, f32[]{:T(128)} %constant.15.clone.1), padding=1_0_1x0_0_0x0_0_0x0_0_0 | pad | bytes 98308
  467.3 1.3 fusion.52
  468.6 0.6 fusion.16
  469.3 0.7 copy.340
  470.0 9.1 %all-to-all-start.1 = ((bf16[32,128,32]{1,2,0:T(8,128)(2,1)}), bf16[32,128,32]{1,2,0:T(8,128)(2,1)S(1)}, u32[]{:S(2)}, u32[]{:S(2)}) async-start(bf16[32,128,32]{1,2,0:T(8,128)(2,1)} %bitcast.27), calls=%async_computation.1 | async-start | bytes 524288 | tf_op jit(solution)/shard_map/all_to_all | solution.py:129
  479.1 2.3 fusion.11
  481.6 0.9 copy.357
  482.4 0.8 copy.356
  483.3 6.9 %all-to-all-done.1 = bf16[32,128,32]{1,2,0:T(8,128)(2,1)S(1)} async-done(((bf16[32,128,32]{1,2,0:T(8,128)(2,1)}), bf16[32,128,32]{1,2,0:T(8,128)(2,1)S(1)}, u32[]{:S(2)}, u32[]{:S(2)}) %all-to-all-start.1) | async-done | bytes 262176 | tf_op jit(solution)/shard_map/all_to_all | solution.py:129
  490.3 0.9 copy.358
  491.2 0.8 copy.354
  (195 shorter events, 14.9 us)
Async XLA Ops:
  0.6 20.3 %copy-start.9 = (f32[64,16]{0,1:T(8,128)S(1)}, f32[64,16]{0,1:T(8,128)}, u32[]{:S(2)}) copy-start(f32[64,16]{0,1:T(8,128)} %param.19) | copy-start | bytes 12292
  0.6 20.3 %copy-start.8 = (f32[64,16]{0,1:T(8,128)S(1)}, f32[64,16]{0,1:T(8,128)}, u32[]{:S(2)}) copy-start(f32[64,16]{0,1:T(8,128)} %param.18) | copy-start | bytes 12292
  0.7 29.6 %copy-start.3 = (f32[64,128]{1,0:T(8,128)S(1)}, f32[64,128]{1,0:T(8,128)}, u32[]{:S(2)}) copy-start(f32[64,128]{1,0:T(8,128)} %param.16) | copy-start | bytes 98308
  2.9 30.5 %copy-start.1 = (bf16[128,1024]{1,0:T(8,128)(2,1)S(1)}, bf16[128,1024]{1,0:T(8,128)(2,1)}, u32[]{:S(2)}) copy-start(bf16[128,1024]{1,0:T(8,128)(2,1)} %param.10) | copy-start | bytes 786436
  3.7 29.9 %copy-start.2 = (bf16[128,1024]{1,0:T(8,128)(2,1)S(1)}, bf16[128,1024]{1,0:T(8,128)(2,1)}, u32[]{:S(2)}) copy-start(bf16[128,1024]{1,0:T(8,128)(2,1)} %param.14) | copy-start | bytes 786436
  3.7 76.8 %all-to-all-start.2 = ((bf16[128,32,32]{0,2,1:T(8,128)(2,1)}), bf16[128,32,32]{0,2,1:T(8,128)(2,1)S(1)}, u32[]{:S(2)}, u32[]{:S(2)}) async-start(bf16[128,32,32]{0,2,1:T(8,128)(2,1)} %bitcast.30), calls=%async_computation.2 | async-start | bytes 524288 | tf_op jit(solution)/shard_map/all_to_all | solution.py:136
  17.6 94.8 %collective-permute-start = (bf16[128,1024]{0,1:T(8,128)(2,1)S(1)}, bf16[128,1024]{0,1:T(8,128)(2,1)}, u32[]{:S(2)}, u32[]{:S(2)}) collective-permute-start(bf16[128,1024]{0,1:T(8,128)(2,1)S(1)} %fusion.22), channel_id=1, source_target_pairs={{0,8},{8,16},{16,24},{24,32},{32,40},{40,48},{48,56},{56,64},{64,7... | collective-permute-start | bytes 786440 | tf_op jit(solution)/shard_map/ppermute | solution.py:21
  21.8 7.3 %copy-start.6 = (f32[2,16]{1,0:T(2,128)}, f32[2,16]{1,0:T(2,128)S(1)}, u32[]{:S(2)}) copy-start(f32[2,16]{1,0:T(2,128)S(1)} %get-tuple-element.106) | copy-start | bytes 388
  33.5 67.0 %copy-start = (f32[2,128,255]{2,1,0:T(8,128)}, f32[2,128,255]{2,1,0:T(8,128)S(1)}, u32[]{:S(2)}) copy-start(f32[2,128,255]{2,1,0:T(8,128)S(1)} %reshape.180) | copy-start | bytes 783364
  85.0 15.8 %copy-start.7 = (f32[2,16]{1,0:T(2,128)S(1)}, f32[2,16]{1,0:T(2,128)}, u32[]{:S(2)}) copy-start(f32[2,16]{1,0:T(2,128)} %copy-done.6) | copy-start | bytes 388
  85.0 15.8 %copy-start.11 = (f32[128]{0:T(128)S(1)}, f32[128]{0:T(128)}, u32[]{:S(2)}) copy-start(f32[128]{0:T(128)} %iota_subtract_fusion) | copy-start | bytes 1540
  100.9 28.4 %copy-start.4 = (f32[1024]{0:T(1024)S(1)}, f32[1024]{0:T(1024)}, u32[]{:S(2)}) copy-start(f32[1024]{0:T(1024)} %param.17) | copy-start | bytes 12292
  103.4 25.9 %all-to-all-start.3 = ((f32[32,128,32]{1,2,0:T(8,128)}), f32[32,128,32]{1,2,0:T(8,128)S(1)}, u32[]{:S(2)}, u32[]{:S(2)}) async-start(f32[32,128,32]{1,2,0:T(8,128)} %bitcast.140), calls=%async_computation.3 | async-start | bytes 1048576 | tf_op jit(solution)/shard_map/all_to_all | solution.py:139
  145.2 308.3 %all-to-all-start = ((bf16[128,32,32]{0,2,1:T(8,128)(2,1)}), bf16[128,32,32]{0,2,1:T(8,128)(2,1)S(1)}, u32[]{:S(2)}, u32[]{:S(2)}) async-start(bf16[128,32,32]{0,2,1:T(8,128)(2,1)} %bitcast.141), calls=%async_computation | async-start | bytes 524288 | tf_op jit(solution)/shard_map/all_to_all | solution.py:126
  206.7 272.4 %collective-permute-start.1 = (bf16[128,1024]{0,1:T(8,128)(2,1)S(1)}, bf16[128,1024]{0,1:T(8,128)(2,1)}, u32[]{:S(2)}, u32[]{:S(2)}) collective-permute-start(bf16[128,1024]{0,1:T(8,128)(2,1)S(1)} %get-tuple-element.66), channel_id=1, source_target_pairs={{8,0},{16,8},{24,16},{32,24},{40,32},{48,40},{56,48},{64,56},{72,6... | collective-permute-start | bytes 786440 | tf_op jit(solution)/shard_map/ppermute | solution.py:21
  311.3 142.1 %copy-start.12 = (f32[128]{0:T(128)S(1)}, f32[128]{0:T(128)}, u32[]{:S(2)}) copy-start(f32[128]{0:T(128)} %iota_subtract_fusion.1) | copy-start | bytes 1540
  311.4 142.7 %copy-start.5 = (f32[2,16]{1,0:T(2,128)S(1)}, f32[2,16]{1,0:T(2,128)}, u32[]{:S(2)}) copy-start(f32[2,16]{1,0:T(2,128)} %get-tuple-element.96) | copy-start | bytes 388
  311.4 142.7 %copy-start.10 = (f32[2,16]{1,0:T(2,128)S(1)}, f32[2,16]{1,0:T(2,128)}, u32[]{:S(2)}) copy-start(f32[2,16]{1,0:T(2,128)} %get-tuple-element.103) | copy-start | bytes 388
  470.0 20.2 %all-to-all-start.1 = ((bf16[32,128,32]{1,2,0:T(8,128)(2,1)}), bf16[32,128,32]{1,2,0:T(8,128)(2,1)S(1)}, u32[]{:S(2)}, u32[]{:S(2)}) async-start(bf16[32,128,32]{1,2,0:T(8,128)(2,1)} %bitcast.27), calls=%async_computation.1 | async-start | bytes 524288 | tf_op jit(solution)/shard_map/all_to_all | solution.py:129
